TPU v7x, 512 devices: a whole 4x8x8 slice. The times are simulated.
512 devices in a mesh: dp: 32 (over y, x), tensor: 16 (over z, core).
Axes of the slice: x: 4, y: 8, z: 8, core: 2. Of those that a mesh axis runs over, the one named last changes fastest.
Arguments:
- grads: bfloat16 [16, 1024, 16384], P(None, 'dp', 'tensor')
- left_slot: int32 [16], replicated, may hold values from 0 to 15, each once
- left_roots: bfloat16 [16, 1024, 1024], P('tensor')
- right_roots: bfloat16 [16, 2048, 1024], P('tensor', 'dp')
Outputs:
- update: bfloat16 [16, 1024, 16384], P(None, 'dp', 'tensor')
Inputs may be any that keep to these rules, and one draw needn't show every extreme that they name: left_slot names every stored left factor exactly once.
All inputs are finite; a program needn't handle non-finite values.
Results may differ from a plain program's by a relative error of at most 0.0049.
Values may be sent and summed in bfloat16 or wider, within the bound.
A program may use at most 64 MiB of HBM per device.

v0:
```python
import jax
import jax.numpy as jnp
from jax import lax
from jax.sharding import PartitionSpec as P

MATS = 2


def spread(block, axis, source):
    block = jnp.where(lax.axis_index(axis) == source, block, jnp.zeros_like(block))
    return lax.psum(block, axis)


def partner(block, axis, bit):
    count = lax.axis_size(axis)
    route = []
    for low in range(count):
        high = low | 1 << bit
        if high != low and high < count:
            route += [(low, high), (high, low)]
    return lax.ppermute(block, axis, route)


def ordered_pair(first_part, second_part, side_bit, axis_number):
    in_order = jnp.concatenate((first_part, second_part), axis_number)
    swapped = jnp.concatenate((second_part, first_part), axis_number)
    return jnp.where(side_bit == 0, in_order, swapped)


def local(grads, left_slot, left_roots, right_roots):
    dp_count = lax.axis_size("dp")
    dp_index = lax.axis_index("dp")
    row_blocks, rows_dev, block_width = grads.shape
    half_width = block_width // 2
    pair_index = dp_index // 2
    side_bit = dp_index % 2
    matrix = pair_index % MATS
    tiles_dev = left_roots.shape[0]
    tile_slot = lax.dynamic_index_in_dim(left_slot, pair_index, 0, keepdims=False)
    own_tile = lax.dynamic_index_in_dim(left_roots, tile_slot % tiles_dev, 0, keepdims=False)
    stacked = lax.all_gather(right_roots, "dp", axis=1, tiled=True)[0]
    right_factor = lax.dynamic_slice_in_dim(stacked, matrix * block_width, block_width, 0)
    pieces = jnp.stack((grads[:, :, :half_width], grads[:, :, half_width:]), axis=1)
    pieces = pieces.reshape(row_blocks * 2, rows_dev, half_width)
    column_half = lax.all_to_all(pieces, "dp", split_axis=0, concat_axis=1, tiled=True)[0]
    left_factor = spread(own_tile, "tensor", tile_slot // tiles_dev)
    mixed_part = jnp.dot(left_factor, column_half, preferred_element_type=jnp.float32).astype(
        jnp.bfloat16
    )
    kept_rows = lax.dynamic_slice_in_dim(mixed_part, side_bit * half_width, half_width, 0)
    sent_rows = lax.dynamic_slice_in_dim(mixed_part, (1 - side_bit) * half_width, half_width, 0)
    received = partner(sent_rows, "dp", 0)
    row_half = ordered_pair(kept_rows, received, side_bit, 1)
    raw_update = jnp.dot(row_half, right_factor, preferred_element_type=jnp.float32)
    own_sums = jnp.stack(
        (jnp.sum(jnp.square(column_half.astype(jnp.float32))), jnp.sum(raw_update * raw_update))
    )
    kept_cols = lax.dynamic_slice_in_dim(raw_update, side_bit * half_width, half_width, 1)
    sent_cols = lax.dynamic_slice_in_dim(raw_update, (1 - side_bit) * half_width, half_width, 1)
    totals = own_sums + partner(own_sums, "dp", 0)
    graft_scale = jnp.sqrt(totals[0] / (totals[1] + 1e-06))
    outgoing = (sent_cols * graft_scale).astype(jnp.bfloat16)
    arrived = partner(outgoing, "dp", 0)
    kept_final = (kept_cols * graft_scale).astype(jnp.bfloat16)
    column_result = ordered_pair(kept_final, arrived, side_bit, 0)
    outgoing_rows = column_result.reshape(dp_count, rows_dev, half_width)
    incoming = lax.all_to_all(outgoing_rows, "dp", split_axis=0, concat_axis=0, tiled=True)
    arranged = incoming.reshape(row_blocks, 2, rows_dev, half_width)
    return jnp.swapaxes(arranged, 1, 2).reshape(row_blocks, rows_dev, block_width)


def solution(mesh):
    in_specs = (P(None, "dp", "tensor"), P(), P("tensor", None, None), P("tensor", "dp", None))
    out_specs = P(None, "dp", "tensor")
    return jax.shard_map(local, mesh=mesh, in_specs=in_specs, out_specs=out_specs, check_vma=False)
```

profile of v0, /device:TPU:2, one launch (start us, length us, event | category | flops | bytes accessed | tf_op | source)
XLA Modules:
  0.0 230.2 jit_solution(8092830772445566729)
XLA Ops:
  7.4 0.0 all-reduce.2.cloned.1.call-start
  7.4 1.2 dynamic_slice.23
  9.3 1.5 select_bitcast_fusion
  10.8 0.0 copy-start
  10.8 0.0 all-reduce.2.cloned.1.call-update
  10.8 0.0 all-gather.2.cloned.1.call-start
  10.8 0.5 all-gather.2.cloned.1.call-update
  11.4 0.6 copy-done
  12.0 0.1 slice_bitcast_fusion.1
  12.1 1.1 pad_maximum_fusion
  13.2 10.3 %all-to-all-start = ((bf16[32,32,512]{2,1,0:T(8,128)(2,1)}), bf16[32,32,512]{2,1,0:T(8,128)(2,1)S(1)}, u32[]{:S(2)}, u32[]{:S(2)}) async-start(bf16[32,32,512]{2,1,0:T(8,128)(2,1)} %bitcast.4), calls=%async_computation | async-start | bytes 2097152 | tf_op jit(solution)/shard_map/all_to_all | solution.py:45
  23.5 115.9 %all-reduce.2.cloned.1.call-done = bf16[1024,1024]{1,0:T(8,128)(2,1)} async-done(((bf16[1024,1024]{1,0:T(8,128)(2,1)}), bf16[1024,1024]{1,0:T(8,128)(2,1)}) %all-reduce.2.cloned.1.call-update) | async-done | bytes 2097168 | tf_op jit(solution)/shard_map/psum | solution.py:11
  139.4 0.0 all-to-all-done
  139.4 2.9 %convolution_convert_fusion = bf16[1024,512]{0,1:T(8,128)(2,1)S(1)} fusion(bf16[1024,1024]{1,0:T(8,128)(2,1)} %all-reduce.2.cloned.1.call-done, bf16[1024,512]{1,0:T(8,128)(2,1)S(1)} %bitcast.25), kind=kOutput, calls=%fused_computation.6 | convolution fusion | flops 1074266112 | bytes 4194304 | tf_op jit(solution)/shard_map/dot_general | solution.py:47
  142.3 0.1 constant_dynamic-slice_fusion.1
  142.4 2.5 %collective-permute-start = (bf16[512,512]{0,1:T(8,128)(2,1)S(1)}, bf16[512,512]{0,1:T(8,128)(2,1)S(1)}, u32[]{:S(2)}, u32[]{:S(2)}) collective-permute-start(bf16[512,512]{0,1:T(8,128)(2,1)S(1)} %get-tuple-element.8), channel_id=1, source_target_pairs={{0,16},{16,0},{32,48},{48,32},{64,80},{80,64},{96,112},{112,96},{1... | collective-permute-start | bytes 1572872 | tf_op jit(solution)/shard_map/ppermute | solution.py:21
  144.9 1.1 multiply_reduce_fusion.1
  146.1 11.4 %collective-permute-done = bf16[512,512]{0,1:T(8,128)(2,1)S(1)} collective-permute-done((bf16[512,512]{0,1:T(8,128)(2,1)S(1)}, bf16[512,512]{0,1:T(8,128)(2,1)S(1)}, u32[]{:S(2)}, u32[]{:S(2)}) %collective-permute-start) | collective-permute-done | bytes 524320 | tf_op jit(solution)/shard_map/ppermute | solution.py:21
  157.5 0.0 all-gather.2.cloned.1.call-done
  157.5 3.8 %multiply_reduce_fusion = (f32[]{:T(128)}, f32[512,1024]{1,0:T(8,128)S(1)}) fusion(bf16[1,2048,1024]{2,1,0:T(8,128)(2,1)} %all-gather.2.cloned.1.call-done, s32[]{:T(128)S(6)} %select_n.78, bf16[512,512]{0,1:T(8,128)(2,1)S(1)} %collective-permute-done, bf16[512,512]{0,1:T(8,128)(2,1)S(1)} %get-tuple-element.7, pred[]{:T(512)S(6)} %eq.11), kind=kOutput, calls=%fused_computation.2 | convolution fusion | flops 1079508992 | bytes 5242889 | tf_op jit(solution)/shard_map/dot_general | solution.py:54
  161.3 1.3 pad_maximum_fusion.1
  162.6 2.4 %collective-permute-start.1 = (f32[2]{0:T(128)S(1)}, f32[2]{0:T(128)S(1)}, u32[]{:S(2)}, u32[]{:S(2)}) collective-permute-start(f32[2]{0:T(128)S(1)} %pad_maximum_fusion.1), channel_id=1, source_target_pairs={{0,16},{16,0},{32,48},{48,32},{64,80},{80,64},{96,112},{112,96},{1... | collective-permute-start | bytes 32 | tf_op jit(solution)/shard_map/ppermute | solution.py:21
  165.1 3.0 %collective-permute-done.1 = f32[2]{0:T(128)S(1)} collective-permute-done((f32[2]{0:T(128)S(1)}, f32[2]{0:T(128)S(1)}, u32[]{:S(2)}, u32[]{:S(2)}) %collective-permute-start.1) | collective-permute-done | bytes 40 | tf_op jit(solution)/shard_map/ppermute | solution.py:21
  168.0 1.3 fusion.14
  169.4 0.6 fusion.11
  171.3 0.3 multiply_convert_fusion.1
  171.6 2.4 %collective-permute-start.2 = (bf16[512,512]{1,0:T(8,128)(2,1)S(1)}, bf16[512,512]{1,0:T(8,128)(2,1)S(1)}, u32[]{:S(2)}, u32[]{:S(2)}) collective-permute-start(bf16[512,512]{1,0:T(8,128)(2,1)S(1)} %get-tuple-element.6), channel_id=1, source_target_pairs={{0,16},{16,0},{32,48},{48,32},{64,80},{80,64},{96,112},{112,96},{1... | collective-permute-start | bytes 1572872 | tf_op jit(solution)/shard_map/ppermute | solution.py:21
  174.1 10.6 %collective-permute-done.2 = bf16[512,512]{1,0:T(8,128)(2,1)S(1)} collective-permute-done((bf16[512,512]{1,0:T(8,128)(2,1)S(1)}, bf16[512,512]{1,0:T(8,128)(2,1)S(1)}, u32[]{:S(2)}, u32[]{:S(2)}) %collective-permute-start.2) | collective-permute-done | bytes 524320 | tf_op jit(solution)/shard_map/ppermute | solution.py:21
  184.7 0.5 maximum_select_fusion.2
  185.1 35.0 %all_to_all.14 = bf16[32,32,512]{2,1,0:T(8,128)(2,1)S(1)} all-to-all(bf16[32,32,512]{2,1,0:T(8,128)(2,1)S(1)} %bitcast.24), channel_id=1, replica_groups=mesh['dp'=32,'tensor'=16] {'dp'}, dimensions={0} | all-to-all | bytes 2097152 | tf_op jit(solution)/shard_map/all_to_all | solution.py:67
  220.2 1.1 copy.8
  221.2 1.5 reshape.28
Async XLA Ops:
  7.4 132.0 %all-reduce.2.cloned.1.call-start = ((), (), s32[]{:S(2)}) async-start(), calls=%async_computation.2 | async-start | bytes 4194304 | tf_op jit(solution)/shard_map/psum | solution.py:11
  10.8 1.2 copy-start
  10.8 146.7 %all-gather.2.cloned.1.call-start = ((), (), s32[]{:S(2)}) async-start(), calls=%async_computation.3 | async-start | bytes 4325376 | tf_op jit(solution)/shard_map/all_gather | solution.py:41
  13.2 126.2 %all-to-all-start = ((bf16[32,32,512]{2,1,0:T(8,128)(2,1)}), bf16[32,32,512]{2,1,0:T(8,128)(2,1)S(1)}, u32[]{:S(2)}, u32[]{:S(2)}) async-start(bf16[32,32,512]{2,1,0:T(8,128)(2,1)} %bitcast.4), calls=%async_computation | async-start | bytes 2097152 | tf_op jit(solution)/shard_map/all_to_all | solution.py:45
  142.4 15.1 %collective-permute-start = (bf16[512,512]{0,1:T(8,128)(2,1)S(1)}, bf16[512,512]{0,1:T(8,128)(2,1)S(1)}, u32[]{:S(2)}, u32[]{:S(2)}) collective-permute-start(bf16[512,512]{0,1:T(8,128)(2,1)S(1)} %get-tuple-element.8), channel_id=1, source_target_pairs={{0,16},{16,0},{32,48},{48,32},{64,80},{80,64},{96,112},{112,96},{1... | collective-permute-start | bytes 1572872 | tf_op jit(solution)/shard_map/ppermute | solution.py:21
  162.6 5.4 %collective-permute-start.1 = (f32[2]{0:T(128)S(1)}, f32[2]{0:T(128)S(1)}, u32[]{:S(2)}, u32[]{:S(2)}) collective-permute-start(f32[2]{0:T(128)S(1)} %pad_maximum_fusion.1), channel_id=1, source_target_pairs={{0,16},{16,0},{32,48},{48,32},{64,80},{80,64},{96,112},{112,96},{1... | collective-permute-start | bytes 32 | tf_op jit(solution)/shard_map/ppermute | solution.py:21
  171.6 13.0 %collective-permute-start.2 = (bf16[512,512]{1,0:T(8,128)(2,1)S(1)}, bf16[512,512]{1,0:T(8,128)(2,1)S(1)}, u32[]{:S(2)}, u32[]{:S(2)}) collective-permute-start(bf16[512,512]{1,0:T(8,128)(2,1)S(1)} %get-tuple-element.6), channel_id=1, source_target_pairs={{0,16},{16,0},{32,48},{48,32},{64,80},{80,64},{96,112},{112,96},{1... | collective-permute-start | bytes 1572872 | tf_op jit(solution)/shard_map/ppermute | solution.py:21
Sparse Core Ops, SparseCore 0:
  10.9 128.4 all-reduce.1
Sparse Core Ops, SparseCore 1:
  14.4 93.9 all-gather.1
where the time goes:
time: 231 us; the launch traced here: 230 us
  waiting for transfers between devices  141 us (61%)
  blocking collectives  35 us (15%)
  starting transfers between devices  17.6 us (8%)
  between operations  17 us (7%)
  other arithmetic  7.16 us (3%)
  matrix products  6.63 us (3%)
  local copies, waits for them, and re-layouts  5.31 us (2%)
    psum x1, waiting for transfers between devices, spread(): return lax.psum(block, axis)  116 us
    all_to_all x1, blocking collectives, local(): lax.all_to_all(outgoing_rows, 'dp', split_axis=0, concat_axis=0, tiled=True)  35 us
    ppermute x3, waiting for transfers between devices, partner(): return lax.ppermute(block, axis, route)  25 us
    all_to_all x1, starting transfers between devices, local(): lax.all_to_all(pieces, 'dp', split_axis=0, concat_axis=1, tiled=True)[0]  10.3 us
    ppermute x3, starting transfers between devices, partner(): return lax.ppermute(block, axis, route)  7.34 us
  transfers between devices with their start and end apart: 6, of which 4 were waited for; matrix products, arithmetic and copies ran while one was open for 2% of the time, Pallas kernels for 0%

commit v1 on v0

v1 whole, which is shorter than its diff:
```python
import functools

import jax
import jax.numpy as jnp
from jax import lax
from jax.experimental import pallas as pl
from jax.experimental.pallas import tpu as pltpu
from jax.sharding import PartitionSpec as P

MESH = pl.DeviceIdType.MESH
CHIPS_X = 4
MATS = 2
MIB = 1 << 20


def kernel(
    nx, ny, nz, chunks,
    slot_ref, g_ref, p_ref, q_ref, o_ref,
    g_stage, g_full, p_half, q_relay, q_stage, q_full, z_buf, u_buf, u_stage, u_recv, sums, sums_in,
    g_send, g_recv, gf_send, gf_recv, p_send, p_sib, p_recv, q_send, q_recv, x_send, x_recv,
    qf_send, qf_recv, s_sem, u_send, u_in,
):
    half = ny // 2
    fold = half // 2
    slots = half * nx
    rows = g_ref.shape[1]
    block = g_ref.shape[2]
    half_block = block // 2
    part = half_block // chunks
    dp = lax.axis_index("dp")
    tensor = lax.axis_index("tensor")
    y, x = dp // nx, dp % nx
    z, core = tensor // 2, tensor % 2
    side, y_low = y // half, y % half
    mine = y_low * nx + x
    own = core == side
    sibling = (dp, z * 2 + 1 - core)
    step = 1 - 2 * core
    z_next = (dp, ((z + step + nz) % nz) * 2 + core)
    z_prev = (dp, ((z - step + nz) % nz) * 2 + core)
    hop = ((z - mine // 2) * step + nz) % nz
    source = (hop == 0) & (core == mine % 2)
    q_core = y_low // fold
    q_own = own & (q_core == core)

    def inverse(slot):
        found = 0
        for k in range(slots):
            found = jnp.where(slot_ref[k] == slot, k, found)
        return found

    def place(offset, sign):
        py = (y_low + sign * (offset // nx) + half) % half
        px = (x + sign * (offset % nx) + nx) % nx
        return py * nx + px

    def partner(pos):
        return (core * slots + pos, z * 2 + side)

    def remote(src, dst, send, recv, device):
        return pltpu.make_async_remote_copy(
            src_ref=src, dst_ref=dst, send_sem=send, recv_sem=recv, device_id=device, device_id_type=MESH
        )

    def arrived(dst, sem):
        pltpu.make_async_copy(dst, dst, sem).wait()

    def g_rows(which, pos):
        return g_full.at[pl.ds(pl.multiple_of((which * slots + pos) * rows, rows), rows), :]

    barrier = pltpu.get_barrier_semaphore()

    def greet(device):
        pl.semaphore_signal(barrier, inc=1, device_id=device, device_id_type=MESH)

    @pl.loop(1, slots)
    def _(offset):
        greet(partner(place(offset, 1)))

    @pl.when(jnp.logical_not(own))
    def _():
        greet(partner(mine))

    @pl.loop(0, half)
    def _(i):
        py = (i // fold) * half + core * fold + i % fold

        @pl.when(jnp.logical_not(q_own & (py == y)))
        def _():
            greet((py * nx + x, z * 2 + side))

    @pl.loop(1, nx)
    def _(ox):
        greet((y * nx + (x + ox) % nx, tensor))

    greet(sibling)
    greet(z_prev)

    @pl.loop(0, slots)
    def _(offset):
        g_stage[offset] = g_ref[inverse(place(offset, 1))]

    pl.semaphore_wait(
        barrier,
        slots - own.astype(jnp.int32) + half - q_own.astype(jnp.int32) + nx - 1 + 2,
    )

    def q_out(i):
        return remote(
            q_ref.at[0], q_relay.at[side, y_low % fold], q_send.at[i], q_recv.at[side, y_low % fold],
            ((core * half + i) * nx + x, z * 2 + q_core),
        )

    @pl.loop(0, half)
    def _(j):
        i = (y_low + j) % half
        keep = q_own & (i == y_low)

        @pl.when(keep)
        def _():
            pltpu.make_async_copy(
                q_ref.at[0], q_relay.at[side, y_low % fold], q_recv.at[side, y_low % fold]
            ).start()

        @pl.when(jnp.logical_not(keep))
        def _():
            q_out(i).start()

    def p_part(t):
        return p_half.at[pl.ds(pl.multiple_of(t * part, part), part), :]

    def p_stored(which, t):
        return p_ref.at[0, pl.ds(pl.multiple_of(which * half_block + t * part, part), part), :]

    def p_side(t):
        return remote(p_stored(1 - core, t), p_part(t), p_sib.at[t], p_recv.at[t], sibling)

    def p_out(t):
        return remote(p_part(t), p_part(t), p_send.at[t], p_recv.at[t], z_next)

    @pl.when(source)
    def _():
        @pl.loop(0, chunks)
        def _(t):
            pltpu.make_async_copy(p_stored(core, t), p_part(t), p_recv.at[t]).start()
            p_side(t).start()

    def g_out(offset):
        return remote(
            g_stage.at[offset], g_rows(side, mine), g_send.at[offset], g_recv.at[offset],
            partner(place(offset, 1)),
        )

    @pl.when(own)
    def _():
        pltpu.make_async_copy(g_stage.at[0], g_rows(side, mine), g_recv.at[0]).start()

    @pl.when(jnp.logical_not(own))
    def _():
        g_out(0).start()

    @pl.loop(1, slots)
    def _(offset):
        g_out(offset).start()

    @pl.loop(0, half)
    def _(i):
        arrived(q_relay.at[i // fold, i % fold], q_recv.at[i // fold, i % fold])

    def x_out(ox):
        return remote(
            q_stage.at[ox], q_full.at[core, :, x], x_send.at[ox], x_recv.at[ox], (y * nx + (x + ox) % nx, tensor)
        )

    @pl.loop(1, nx)
    def _(ox):
        q_stage[ox] = q_relay[inverse(y_low * nx + (x + ox) % nx) % MATS]
        x_out(ox).start()

    q_full[core, :, x] = q_relay[inverse(mine) % MATS]

    def q_forward(ox):
        piece = q_full.at[core, :, (x - ox + nx) % nx]
        return remote(piece, piece, qf_send.at[ox], qf_recv.at[ox], sibling)

    q_forward(0).start()

    def g_forward(offset):
        piece = g_rows(core, place(offset, -1))
        return remote(piece, piece, gf_send.at[offset], gf_recv.at[offset], sibling)

    steps = max(chunks, slots)

    def pass_on(t, total):
        if chunks == steps:
            arrived(p_part(t), p_recv.at[t])

            @pl.when(hop < nz - 1)
            def _():
                p_out(t).start()

        pos = place(t, -1)
        arrived(g_rows(core, pos), g_recv.at[t])
        g_forward(t).start()
        values = g_rows(core, pos)[...].astype(jnp.float32)
        return total + jnp.sum((values * values).reshape(-1, 8, 128), axis=0)

    sums[0] = lax.fori_loop(0, slots, pass_on, jnp.zeros((8, 128), jnp.float32))

    @pl.loop(1, nx)
    def _(ox):
        arrived(q_full.at[core, :, (x - ox + nx) % nx], x_recv.at[ox])
        q_forward(ox).start()

    @pl.loop(0, slots)
    def _(offset):
        arrived(g_rows(1 - core, place(offset, -1)), gf_recv.at[offset])

    width = 256

    @pl.loop(0, block // width)
    def _(n):
        cols = pl.ds(pl.multiple_of(n * width, width), width)
        z_buf[:, cols] = jnp.dot(p_half[...], g_full[:, cols], preferred_element_type=jnp.float32).astype(
            jnp.bfloat16
        )

    @pl.loop(0, nx)
    def _(ox):
        arrived(q_full.at[1 - core, :, (x - ox + nx) % nx], qf_recv.at[ox])

    def right(n, total):
        cols = pl.ds(pl.multiple_of(n * width, width), width)
        factor = q_full[:, :, :, :, cols].reshape(block, width)
        value = jnp.dot(z_buf[...], factor, preferred_element_type=jnp.float32)
        u_buf[:, cols] = value
        return total + jnp.sum((value * value).reshape(-1, 8, 128), axis=0)

    sums[1] = lax.fori_loop(0, block // width, right, jnp.zeros((8, 128), jnp.float32))

    exchange = remote(sums, sums_in, s_sem.at[0], s_sem.at[1], sibling)
    exchange.start()
    exchange.wait()
    graft = jnp.sqrt(jnp.sum(sums[0] + sums_in[0]) / (jnp.sum(sums[1] + sums_in[1]) + 1e-06))

    def u_out(offset):
        return remote(
            u_stage.at[offset], u_recv.at[mine], u_send.at[offset], u_in.at[offset],
            partner(place(offset, -1)),
        )

    def u_scaled(offset):
        first = pl.multiple_of(place(offset, -1) * rows, rows)
        return (u_buf[pl.ds(first, rows), :] * graft).astype(jnp.bfloat16)

    u_stage[0] = u_scaled(0)

    @pl.when(own)
    def _():
        pltpu.make_async_copy(u_stage.at[0], u_recv.at[mine], u_in.at[0]).start()

    @pl.when(jnp.logical_not(own))
    def _():
        u_out(0).start()

    @pl.loop(1, slots)
    def _(offset):
        u_stage[offset] = u_scaled(offset)
        u_out(offset).start()

    @pl.when(jnp.logical_not(own))
    def _():
        g_out(0).wait_send()

    @pl.loop(1, slots)
    def _(offset):
        g_out(offset).wait_send()

    @pl.loop(0, half)
    def _(i):
        @pl.when(jnp.logical_not(q_own & (i == y_low)))
        def _():
            q_out(i).wait_send()

    @pl.loop(1, nx)
    def _(ox):
        x_out(ox).wait_send()

    @pl.loop(0, nx)
    def _(ox):
        q_forward(ox).wait_send()

    @pl.loop(0, slots)
    def _(offset):
        g_forward(offset).wait_send()

    @pl.when(source)
    def _():
        @pl.loop(0, chunks)
        def _(t):
            p_side(t).wait_send()

    @pl.when(hop < nz - 1)
    def _():
        @pl.loop(0, chunks)
        def _(t):
            p_out(t).wait_send()

    @pl.loop(0, slots)
    def _(offset):
        arrived(u_recv.at[place(offset, 1)], u_in.at[offset])

    @pl.when(jnp.logical_not(own))
    def _():
        u_out(0).wait_send()

    @pl.loop(1, slots)
    def _(offset):
        u_out(offset).wait_send()

    @pl.loop(0, slots)
    def _(k):
        o_ref[k] = u_recv[slot_ref[k]]


def local(nx, ny, nz, grads, left_slot, left_roots, right_roots):
    slots, rows, block = grads.shape
    half = ny // 2
    fold = half // 2
    chunks = slots
    shard = right_roots.shape[1]
    bf16, f32 = jnp.bfloat16, jnp.float32
    dma = pltpu.SemaphoreType.DMA
    vmem = pl.BlockSpec(memory_space=pltpu.VMEM)
    anywhere = pl.BlockSpec(memory_space=pl.ANY)
    return pl.pallas_call(
        functools.partial(kernel, nx, ny, nz, chunks),
        out_shape=jax.ShapeDtypeStruct(grads.shape, bf16),
        in_specs=[pl.BlockSpec(memory_space=pltpu.SMEM), vmem, anywhere, anywhere],
        out_specs=vmem,
        scratch_shapes=[
            pltpu.VMEM((slots, rows, block), bf16),
            pltpu.VMEM((block, block), bf16),
            pltpu.VMEM((block // 2, block), bf16),
            pltpu.VMEM((MATS, fold, shard, block), bf16),
            pltpu.VMEM((nx, fold, shard, block), bf16),
            pltpu.VMEM((2, fold, nx, shard, block), bf16),
            pltpu.VMEM((block // 2, block), bf16),
            pltpu.VMEM((block // 2, block), f32),
            pltpu.VMEM((slots, rows, block), bf16),
            pltpu.VMEM((slots, rows, block), bf16),
            pltpu.VMEM((2, 8, 128), f32),
            pltpu.VMEM((2, 8, 128), f32),
            dma((slots,)), dma((slots,)), dma((slots,)), dma((slots,)),
            dma((chunks,)), dma((chunks,)), dma((chunks,)),
            dma((half,)), dma((MATS, fold)),
            dma((nx,)), dma((nx,)), dma((nx,)), dma((nx,)),
            dma((2,)),
            dma((slots,)), dma((slots,)),
        ],
        compiler_params=pltpu.CompilerParams(
            collective_id=0, has_side_effects=True, vmem_limit_bytes=40 * MIB
        ),
        cost_estimate=pl.CostEstimate(
            flops=2 * block * block * block, bytes_accessed=16 * MIB, transcendentals=0
        ),
        name="precondition",
    )(left_slot, grads, left_roots, right_roots)


def solution(mesh):
    nx = CHIPS_X
    ny = mesh.shape["dp"] // nx
    nz = mesh.shape["tensor"] // 2
    in_specs = (P(None, "dp", "tensor"), P(), P("tensor", None, None), P("tensor", "dp", None))
    out_specs = P(None, "dp", "tensor")
    return jax.shard_map(
        functools.partial(local, nx, ny, nz), mesh=mesh, in_specs=in_specs, out_specs=out_specs, check_vma=False
    )
```

time: 231 us -> 110 us (0.48)
  waiting for transfers between devices: 141 us -> 0 us
  Pallas kernels: 0 us -> 105 us
  blocking collectives: 35 us -> 0 us
  starting transfers between devices: 17.6 us -> 0 us
  between operations: 17 us -> 0.01 us
  other arithmetic: 7.16 us -> 0 us
  matrix products: 6.63 us -> 0 us
    psum x1 -> x0, waiting for transfers between devices: 116 us -> none  [spread(): return lax.psum(block, axis)]
    pallas_call x0 -> x1, Pallas kernels: none -> 105 us  [local(): pl.pallas_call(functools.partial(kernel, nx, ny, nz, chunks), out_shape=j...]
    all_to_all x1 -> x0, blocking collectives: 35 us -> none  [local(): lax.all_to_all(outgoing_rows, 'dp', split_axis=0, concat_axis=0, tiled=True)]
    ppermute x3 -> x0, waiting for transfers between devices: 25 us -> none  [partner(): return lax.ppermute(block, axis, route)]
    all_to_all x1 -> x0, starting transfers between devices: 10.3 us -> none  [local(): lax.all_to_all(pieces, 'dp', split_axis=0, concat_axis=1, tiled=True)[0]]
    ppermute x3 -> x0, starting transfers between devices: 7.34 us -> none  [partner(): return lax.ppermute(block, axis, route)]
    dot_general x2 -> x0, matrix products: 6.63 us -> none  [the longest x1 3.75 us: local(): jnp.dot(row_half, right_factor, preferred_element_type=jnp.float32)]
    unnamed x2 -> x9, local copies, waits for them, and re-layouts: 0.62 us -> 5.35 us
  transfers between devices with their start and end apart: 6 -> 0, of which waited for: 4 -> 0; matrix products, arithmetic and copies ran while one was open for 2% -> 0% of each run, Pallas kernels for 0% -> 0%
where the time goes in v1:
time: 110 us
  Pallas kernels  105 us (95%)
  local copies, waits for them, and re-layouts  5.35 us (5%)
    pallas_call x1, Pallas kernels, local(): pl.pallas_call(functools.partial(kernel, nx, ny, nz, chunks), out_shape=j...  105 us
    unnamed x9, local copies, waits for them, and re-layouts  5.35 us

profile of v1, /device:TPU:2, one launch (start us, length us, event | category | flops | bytes accessed | tf_op | source)
XLA Modules:
  0.0 110.1 jit_solution(14484309731865004145)
XLA Ops:
  0.0 0.0 copy-start
  0.0 1.6 %copy-done = bf16[1,1024,1024]{2,1,0:T(8,128)(2,1)S(1)} copy-done((bf16[1,1024,1024]{2,1,0:T(8,128)(2,1)S(1)}, bf16[1,1024,1024]{2,1,0:T(8,128)(2,1)}, u32[]{:S(2)}) %copy-start) | copy-done | bytes 2097176
  1.6 0.0 copy-start.1
  1.6 1.2 %copy-done.1 = bf16[16,32,1024]{2,1,0:T(8,128)(2,1)S(1)} copy-done((bf16[16,32,1024]{2,1,0:T(8,128)(2,1)S(1)}, bf16[16,32,1024]{2,1,0:T(8,128)(2,1)}, u32[]{:S(2)}) %copy-start.1) | copy-done | bytes 1048600
  2.8 0.0 copy-start.2
  2.8 0.9 copy-done.2
  3.7 0.0 copy-start.3
  3.7 0.7 copy-done.3
  4.4 104.7 %precondition.1 = bf16[16,32,1024]{2,1,0:T(8,128)(2,1)S(1)} custom-call(s32[16]{0:T(128)S(1)} %copy-done.3, bf16[16,32,1024]{2,1,0:T(8,128)(2,1)S(1)} %copy-done.1, bf16[1,1024,1024]{2,1,0:T(8,128)(2,1)S(1)} %copy-done, bf16[1,64,1024]{2,1,0:T(8,128)(2,1)S(1)} %copy-done.2), custom_call_target="tpu_custom_call" | custom-call | flops 2147483648 | bytes 16777216 | tf_op jit(solution)/shard_map/precondition/pallas_call | solution.py:336
  109.1 1.0 copy.6
Async XLA Ops:
  0.0 1.6 %copy-start = (bf16[1,1024,1024]{2,1,0:T(8,128)(2,1)S(1)}, bf16[1,1024,1024]{2,1,0:T(8,128)(2,1)}, u32[]{:S(2)}) copy-start(bf16[1,1024,1024]{2,1,0:T(8,128)(2,1)} %p_ref.1) | copy-start | bytes 6291460
  1.6 1.2 %copy-start.1 = (bf16[16,32,1024]{2,1,0:T(8,128)(2,1)S(1)}, bf16[16,32,1024]{2,1,0:T(8,128)(2,1)}, u32[]{:S(2)}) copy-start(bf16[16,32,1024]{2,1,0:T(8,128)(2,1)} %g_ref.1) | copy-start | bytes 3145732
  2.8 0.9 copy-start.2
  3.7 0.7 copy-start.3

commit v2 on v1

v2 whole, which is shorter than its diff:
```python
import functools

import jax
import jax.numpy as jnp
from jax import lax
from jax.experimental import pallas as pl
from jax.experimental.pallas import tpu as pltpu
from jax.sharding import PartitionSpec as P

MESH = pl.DeviceIdType.MESH
CHIPS_X = 4
MATS = 2
MIB = 1 << 20
PIECES = 2


def kernel(
    nx, ny, nz, chunks,
    slot_ref, g_hbm, p_ref, q_ref, o_ref,
    g_ref, g_stage, g_full, p_half, q_relay_first, q_relay_last, q_stage, q_full, z_sum, z_buf, u_buf, u_stage, u_recv, sums, sums_in,
    g_send, g_recv, gf_send, gf_recv, p_send, p_sib, p_recv, q_send, q_recv, x_send, x_recv,
    qf_send, qf_recv, s_sem, u_send, u_in, in_sem,
):
    half = ny // 2
    fold = half // 2
    slots = half * nx
    rows = g_ref.shape[1]
    block = g_ref.shape[2]
    half_block = block // 2
    part = half_block // chunks
    dp = lax.axis_index("dp")
    tensor = lax.axis_index("tensor")
    y, x = dp // nx, dp % nx
    z, core = tensor // 2, tensor % 2
    side, y_low = y // half, y % half
    mine = y_low * nx + x
    own = core == side
    sibling = (dp, z * 2 + 1 - core)
    step = 1 - 2 * core
    z_next = (dp, ((z + step + nz) % nz) * 2 + core)
    z_prev = (dp, ((z - step + nz) % nz) * 2 + core)
    hop = ((z - mine // 2) * step + nz) % nz
    source = (hop == 0) & (core == mine % 2)
    q_core = y_low // fold
    q_own = own & (q_core == core)

    def inverse(slot):
        found = 0
        for k in range(slots):
            found = jnp.where(slot_ref[k] == slot, k, found)
        return found

    def place(offset, sign):
        py = (y_low + sign * (offset // nx) + half) % half
        px = (x + sign * (offset % nx) + nx) % nx
        return py * nx + px

    pairs = nx // 2
    wave_size = slots // 2

    def target(w):
        wave, i = w // wave_size, w % wave_size
        py = (y_low + i // pairs) % half
        px = 2 * ((x // 2 + i) % pairs) + (wave + py) % 2
        return py * nx + px

    def sender(e):
        i = e // 2
        sy = (y_low - i // pairs + half) % half
        sx = 2 * ((x // 2 - i % pairs + pairs) % pairs) + e % 2
        return sy * nx + sx

    def partner(pos):
        return (core * slots + pos, z * 2 + side)

    def remote(src, dst, send, recv, device):
        return pltpu.make_async_remote_copy(
            src_ref=src, dst_ref=dst, send_sem=send, recv_sem=recv, device_id=device, device_id_type=MESH
        )

    def arrived(dst, sem):
        pltpu.make_async_copy(dst, dst, sem).wait()

    def g_rows(which, pos):
        return g_full.at[pl.ds(pl.multiple_of((which * slots + pos) * rows, rows), rows), :]

    own_rows = pltpu.make_async_copy(g_hbm, g_ref, in_sem)
    own_rows.start()

    barrier = pltpu.get_barrier_semaphore()

    def greet(device):
        pl.semaphore_signal(barrier, inc=1, device_id=device, device_id_type=MESH)

    @pl.loop(1, slots)
    def _(offset):
        greet(partner(place(offset, 1)))

    @pl.when(jnp.logical_not(own))
    def _():
        greet(partner(mine))

    @pl.loop(0, half)
    def _(i):
        py = (i // fold) * half + core * fold + i % fold

        @pl.when(jnp.logical_not(q_own & (py == y)))
        def _():
            greet((py * nx + x, z * 2 + side))

    @pl.loop(1, nx)
    def _(ox):
        greet((y * nx + (x + ox) % nx, tensor))

    greet(sibling)
    greet(z_prev)

    own_rows.wait()

    @pl.loop(0, slots)
    def _(offset):
        g_stage[offset] = g_ref[inverse(target(offset))]

    pl.semaphore_wait(
        barrier,
        slots - own.astype(jnp.int32) + half - q_own.astype(jnp.int32) + nx - 1 + 2,
    )

    shard = q_ref.shape[1]
    pieces = PIECES
    piece = shard // pieces
    q_relay = (q_relay_first, q_relay_last)

    def q_span(part):
        return pl.ds(part * piece, piece)

    def q_spot(hh, i, part):
        return q_relay[part].at[hh, i]

    def q_out(i, part):
        return remote(
            q_ref.at[0, q_span(part)], q_spot(side, y_low % fold, part), q_send.at[i, part],
            q_recv.at[side, y_low % fold, part], ((core * half + i) * nx + x, z * 2 + q_core),
        )

    def send_q():
        for part in range(pieces):

            @pl.loop(0, half)
            def _(j):
                i = (y_low + j) % half
                keep = q_own & (i == y_low)

                @pl.when(keep)
                def _():
                    pltpu.make_async_copy(
                        q_ref.at[0, q_span(part)], q_spot(side, y_low % fold, part),
                        q_recv.at[side, y_low % fold, part],
                    ).start()

                @pl.when(jnp.logical_not(keep))
                def _():
                    q_out(i, part).start()

    def p_part(t):
        return p_half.at[pl.ds(pl.multiple_of(t * part, part), part), :]

    def p_stored(which, t):
        return p_ref.at[0, pl.ds(pl.multiple_of(which * half_block + t * part, part), part), :]

    def p_side(t):
        return remote(p_stored(1 - core, t), p_part(t), p_sib.at[t], p_recv.at[t], sibling)

    def p_out(t):
        return remote(p_part(t), p_part(t), p_send.at[t], p_recv.at[t], z_next)

    def p_first(t):
        return remote(p_stored(core, t), p_part(t), p_send.at[t], p_recv.at[t], z_next)

    passes = (hop < nz - 1) & jnp.logical_not(source)

    def send_p():
        @pl.when(source)
        def _():
            @pl.loop(0, chunks)
            def _(t):
                p_first(t).start()
                p_side(t).start()
                pltpu.make_async_copy(p_stored(core, t), p_part(t), p_recv.at[t]).start()

    def pass_p(first, last):
        @pl.loop(first, last)
        def _(t):
            arrived(p_part(t), p_recv.at[t])

            @pl.when(passes)
            def _():
                p_out(t).start()

    def g_out(w):
        return remote(
            g_stage.at[w], g_rows(side, mine), g_send.at[w], g_recv.at[2 * (w % wave_size) + x % 2],
            partner(target(w)),
        )

    def send_g(first, last):
        @pl.loop(first, last)
        def _(w):
            keep = own & (target(w) == mine)

            @pl.when(keep)
            def _():
                pltpu.make_async_copy(g_stage.at[w], g_rows(side, mine), g_recv.at[x % 2]).start()

            @pl.when(jnp.logical_not(keep))
            def _():
                g_out(w).start()

    def q_part(which, column, part):
        return q_full.at[which, :, column, q_span(part)]

    def x_out(ox, part):
        return remote(
            q_stage.at[ox, :, q_span(part)], q_part(core, x, part), x_send.at[ox, part], x_recv.at[ox, part],
            (y * nx + (x + ox) % nx, tensor),
        )

    def q_forward(ox, part):
        spot = q_part(core, (x - ox + nx) % nx, part)
        return remote(spot, spot, qf_send.at[ox, part], qf_recv.at[ox, part], sibling)

    def turn_q(part):
        @pl.loop(0, half)
        def _(i):
            arrived(q_spot(i // fold, i % fold, part), q_recv.at[i // fold, i % fold, part])

        @pl.loop(1, nx)
        def _(ox):
            q_stage[ox, :, q_span(part)] = q_relay[part][inverse(y_low * nx + (x + ox) % nx) % MATS]
            x_out(ox, part).start()

        q_full[core, :, x, q_span(part)] = q_relay[part][inverse(mine) % MATS]
        q_forward(0, part).start()

    def pass_q():
        for part in range(pieces):

            @pl.loop(1, nx)
            def _(ox):
                arrived(q_part(core, (x - ox + nx) % nx, part), x_recv.at[ox, part])
                q_forward(ox, part).start()

    def take_q():
        for part in range(pieces):

            @pl.loop(0, nx)
            def _(ox):
                arrived(q_part(1 - core, (x - ox + nx) % nx, part), qf_recv.at[ox, part])

    def g_forward(offset):
        piece = g_rows(core, sender(offset))
        return remote(piece, piece, gf_send.at[offset], gf_recv.at[offset], sibling)

    def pass_g(first, last, total):
        def one(t, total):
            pos = sender(t)
            arrived(g_rows(core, pos), g_recv.at[t])
            g_forward(t).start()
            values = g_rows(core, pos)[...].astype(jnp.float32)
            return total + jnp.sum((values * values).reshape(-1, 8, 128), axis=0)

        return lax.fori_loop(first, last, one, total)

    def take_g(first, last):
        @pl.loop(first, last)
        def _(offset):
            arrived(g_rows(1 - core, sender(offset)), gf_recv.at[offset])

    width = 256

    span = rows * nx

    def left_part(which, first, begin, end):
        tops = [
            pl.multiple_of((which * slots + ((y_low - first - i + half) % half) * nx) * rows, span) for i in range(2)
        ]
        left = jnp.concatenate([p_half[:, pl.ds(top, span)] for top in tops], axis=1)

        @pl.loop(0, block // width)
        def _(n):
            cols = pl.ds(pl.multiple_of(n * width, width), width)
            right = jnp.concatenate([g_full[pl.ds(top, span), cols] for top in tops], axis=0)
            value = jnp.dot(left, right, preferred_element_type=jnp.float32)
            if not begin:
                value = z_sum[:, cols] + value
            if end:
                z_buf[:, cols] = value.astype(jnp.bfloat16)
            else:
                z_sum[:, cols] = value

    def right_product():
        def right(n, total):
            cols = pl.ds(pl.multiple_of(n * width, width), width)
            factor = q_full[:, :, :, :, cols].reshape(block, width)
            value = jnp.dot(z_buf[...], factor, preferred_element_type=jnp.float32)
            u_buf[:, cols] = value
            return total + jnp.sum((value * value).reshape(-1, 8, 128), axis=0)

        return lax.fori_loop(0, block // width, right, jnp.zeros((8, 128), jnp.float32))

    def u_out(offset):
        return remote(
            u_stage.at[offset], u_recv.at[mine], u_send.at[offset], u_in.at[offset],
            partner(place(offset, -1)),
        )

    def send_u(graft):
        def scaled(offset):
            first = pl.multiple_of(place(offset, -1) * rows, rows)
            return (u_buf[pl.ds(first, rows), :] * graft).astype(jnp.bfloat16)

        u_stage[0] = scaled(0)

        @pl.when(own)
        def _():
            pltpu.make_async_copy(u_stage.at[0], u_recv.at[mine], u_in.at[0]).start()

        @pl.when(jnp.logical_not(own))
        def _():
            u_out(0).start()

        @pl.loop(1, slots)
        def _(offset):
            u_stage[offset] = scaled(offset)
            u_out(offset).start()

    def sent_g(first, last):
        @pl.loop(first, last)
        def _(w):
            @pl.when(jnp.logical_not(own & (target(w) == mine)))
            def _():
                g_out(w).wait_send()

    def left_g():
        @pl.loop(0, slots)
        def _(offset):
            g_forward(offset).wait_send()

    def left_q():
        for part in range(pieces):

            @pl.loop(0, half)
            def _(i):
                @pl.when(jnp.logical_not(q_own & (i == y_low)))
                def _():
                    q_out(i, part).wait_send()

            @pl.loop(1, nx)
            def _(ox):
                x_out(ox, part).wait_send()

            @pl.loop(0, nx)
            def _(ox):
                q_forward(ox, part).wait_send()

    def left_p():
        @pl.when(source)
        def _():
            @pl.loop(0, chunks)
            def _(t):
                p_side(t).wait_send()

        @pl.when(hop < nz - 1)
        def _():
            @pl.loop(0, chunks)
            def _(t):
                p_out(t).wait_send()

    def take_u():
        @pl.loop(0, slots)
        def _(offset):
            arrived(u_recv.at[place(offset, 1)], u_in.at[offset])

        @pl.when(jnp.logical_not(own))
        def _():
            u_out(0).wait_send()

        @pl.loop(1, slots)
        def _(offset):
            u_out(offset).wait_send()

    send_q()
    send_p()
    send_g(0, wave_size // 2)
    first_cut = jnp.clip((9 - 3 * hop) * 4 // 3 * chunks // 16, 0, chunks)
    second_cut = jnp.clip((15 - 3 * hop) * 4 // 3 * chunks // 16, first_cut, chunks)
    pass_p(0, first_cut)
    turn_q(0)
    send_g(wave_size // 2, wave_size)
    pass_p(first_cut, second_cut)
    turn_q(1)
    send_g(wave_size, slots)
    pass_p(second_cut, chunks)
    zero = jnp.zeros((8, 128), jnp.float32)
    pass_q()
    middle = slots // 2
    part_sum = pass_g(0, middle, zero)
    left_part(core, 0, True, False)
    take_g(0, middle)
    left_part(1 - core, 0, False, False)
    sums[0] = pass_g(middle, slots, part_sum)
    left_part(core, 2, False, False)
    take_g(middle, slots)
    left_part(1 - core, 2, False, True)
    take_q()
    sums[1] = right_product()
    exchange = remote(sums, sums_in, s_sem.at[0], s_sem.at[1], sibling)
    exchange.start()
    exchange.wait()
    graft = jnp.sqrt(jnp.sum(sums[0] + sums_in[0]) / (jnp.sum(sums[1] + sums_in[1]) + 1e-06))
    send_u(graft)
    sent_g(0, slots)
    left_g()
    left_q()
    left_p()
    take_u()

    @pl.loop(0, slots)
    def _(k):
        o_ref[k] = u_recv[slot_ref[k]]


def local(nx, ny, nz, grads, left_slot, left_roots, right_roots):
    slots, rows, block = grads.shape
    half = ny // 2
    fold = half // 2
    chunks = slots
    pieces = PIECES
    shard = right_roots.shape[1]
    bf16, f32 = jnp.bfloat16, jnp.float32
    dma = pltpu.SemaphoreType.DMA
    vmem = pl.BlockSpec(memory_space=pltpu.VMEM)
    hbm = pl.BlockSpec(memory_space=pl.ANY)
    return pl.pallas_call(
        functools.partial(kernel, nx, ny, nz, chunks),
        out_shape=jax.ShapeDtypeStruct(grads.shape, bf16),
        in_specs=[pl.BlockSpec(memory_space=pltpu.SMEM), hbm, hbm, hbm],
        out_specs=vmem,
        scratch_shapes=[
            pltpu.VMEM((slots, rows, block), bf16),
            pltpu.VMEM((slots, rows, block), bf16),
            pltpu.VMEM((block, block), bf16),
            pltpu.VMEM((block // 2, block), bf16),
            pltpu.VMEM((MATS, fold, shard // pieces, block), bf16),
            pltpu.VMEM((MATS, fold, shard // pieces, block), bf16),
            pltpu.VMEM((nx, fold, shard, block), bf16),
            pltpu.VMEM((2, fold, nx, shard, block), bf16),
            pltpu.VMEM((block // 2, block), f32),
            pltpu.VMEM((block // 2, block), bf16),
            pltpu.VMEM((block // 2, block), f32),
            pltpu.VMEM((slots, rows, block), bf16),
            pltpu.VMEM((slots, rows, block), bf16),
            pltpu.VMEM((2, 8, 128), f32),
            pltpu.VMEM((2, 8, 128), f32),
            dma((slots,)), dma((slots,)), dma((slots,)), dma((slots,)),
            dma((chunks,)), dma((chunks,)), dma((chunks,)),
            dma((half, pieces)), dma((MATS, fold, pieces)),
            dma((nx, pieces)), dma((nx, pieces)), dma((nx, pieces)), dma((nx, pieces)),
            dma((2,)),
            dma((slots,)), dma((slots,)), dma,
        ],
        compiler_params=pltpu.CompilerParams(
            collective_id=0, has_side_effects=True, vmem_limit_bytes=60 * MIB
        ),
        cost_estimate=pl.CostEstimate(
            flops=2 * block * block * block, bytes_accessed=16 * MIB, transcendentals=0
        ),
        name="precondition",
    )(left_slot, grads, left_roots, right_roots)


def solution(mesh):
    nx = CHIPS_X
    ny = mesh.shape["dp"] // nx
    nz = mesh.shape["tensor"] // 2
    in_specs = (P(None, "dp", "tensor"), P(), P("tensor", None, None), P("tensor", "dp", None))
    out_specs = P(None, "dp", "tensor")
    return jax.shard_map(
        functools.partial(local, nx, ny, nz), mesh=mesh, in_specs=in_specs, out_specs=out_specs, check_vma=False
    )
```

time: 110 us -> 89.8 us (0.82)
  the two profiles are of different devices: /device:TPU:2 before, /device:TPU:9 now
where the time goes in v2:
time: 89.8 us; the launch traced here: 89.5 us
  Pallas kernels  87.2 us (97%)
  local copies, waits for them, and re-layouts  2.29 us (3%)
    pallas_call x1, Pallas kernels, local(): pl.pallas_call(functools.partial(kernel, nx, ny, nz, chunks), out_shape=j...  87.2 us
    unnamed x1, local copies, waits for them, and re-layouts  2.29 us

profile of v2, /device:TPU:9, one launch (start us, length us, event | category | flops | bytes accessed | tf_op | source)
XLA Modules:
  0.0 89.5 jit_solution(1634666424159446702)
XLA Ops:
  0.0 87.2 %precondition.1 = bf16[16,32,1024]{2,1,0:T(8,128)(2,1)} custom-call(s32[16]{0:T(128)} %slot_ref.1, bf16[16,32,1024]{2,1,0:T(8,128)(2,1)} %g_hbm.1, bf16[1,1024,1024]{2,1,0:T(8,128)(2,1)} %p_ref.1, bf16[1,64,1024]{2,1,0:T(8,128)(2,1)} %q_ref.1), custom_call_target="tpu_custom_call" | custom-call | flops 2147483648 | bytes 16777216 | tf_op jit(solution)/shard_map/precondition/pallas_call | solution.py:444
  87.2 2.3 %copy.6 = bf16[16,32,1024]{2,1,0:T(8,128)(2,1)} copy(bf16[16,32,1024]{2,1,0:T(8,128)(2,1)} %precondition.1) | data formatting | bytes 2097152

commit v3 on v2

--- a/solution.py
+++ b/solution.py
@@ -330,7 +330,8 @@
             u_out(0).start()
 
         @pl.loop(1, slots)
-        def _(offset):
+        def _(turn):
+            offset = (turn + 2 * nx - 1) % (slots - 1) + 1
             u_stage[offset] = scaled(offset)
             u_out(offset).start()
 
@@ -402,10 +403,10 @@
     send_g(wave_size, slots)
     pass_p(second_cut, chunks)
     zero = jnp.zeros((8, 128), jnp.float32)
-    pass_q()
     middle = slots // 2
     part_sum = pass_g(0, middle, zero)
     left_part(core, 0, True, False)
+    pass_q()
     take_g(0, middle)
     left_part(1 - core, 0, False, False)
     sums[0] = pass_g(middle, slots, part_sum)

time: 89.8 us -> 87.3 us (0.972)
  the two profiles are of different devices: /device:TPU:9 before, /device:TPU:57 now
where the time goes in v3:
time: 87.3 us; the launch traced here: 87.1 us
  Pallas kernels  84.8 us (97%)
  local copies, waits for them, and re-layouts  2.29 us (3%)
    pallas_call x1, Pallas kernels, local(): pl.pallas_call(functools.partial(kernel, nx, ny, nz, chunks), out_shape=j...  84.8 us
    unnamed x1, local copies, waits for them, and re-layouts  2.29 us

profile of v3, /device:TPU:57, one launch (start us, length us, event | category | flops | bytes accessed | tf_op | source)
XLA Modules:
  0.0 87.1 jit_solution(14620856417840799730)
XLA Ops:
  0.0 84.8 %precondition.1 = bf16[16,32,1024]{2,1,0:T(8,128)(2,1)} custom-call(s32[16]{0:T(128)} %slot_ref.1, bf16[16,32,1024]{2,1,0:T(8,128)(2,1)} %g_hbm.1, bf16[1,1024,1024]{2,1,0:T(8,128)(2,1)} %p_ref.1, bf16[1,64,1024]{2,1,0:T(8,128)(2,1)} %q_ref.1), custom_call_target="tpu_custom_call" | custom-call | flops 2147483648 | bytes 16777216 | tf_op jit(solution)/shard_map/precondition/pallas_call | solution.py:445
  84.8 2.3 %copy.6 = bf16[16,32,1024]{2,1,0:T(8,128)(2,1)} copy(bf16[16,32,1024]{2,1,0:T(8,128)(2,1)} %precondition.1) | data formatting | bytes 2097152

commit v4 on v3

--- a/solution.py
+++ b/solution.py
@@ -60,13 +60,13 @@
 
     def target(w):
         wave, i = w // wave_size, w % wave_size
-        py = (y_low + i // pairs) % half
+        py = (y_low + i // pairs + half // 2) % half
         px = 2 * ((x // 2 + i) % pairs) + (wave + py) % 2
         return py * nx + px
 
     def sender(e):
         i = e // 2
-        sy = (y_low - i // pairs + half) % half
+        sy = (y_low - i // pairs + half + half // 2) % half
         sx = 2 * ((x // 2 - i % pairs + pairs) % pairs) + e % 2
         return sy * nx + sx
 
@@ -210,7 +210,7 @@
 
             @pl.when(keep)
             def _():
-                pltpu.make_async_copy(g_stage.at[w], g_rows(side, mine), g_recv.at[x % 2]).start()
+                pltpu.make_async_copy(g_stage.at[w], g_rows(side, mine), g_recv.at[2 * (w % wave_size) + x % 2]).start()
 
             @pl.when(jnp.logical_not(keep))
             def _():
@@ -282,7 +282,7 @@
 
     def left_part(which, first, begin, end):
         tops = [
-            pl.multiple_of((which * slots + ((y_low - first - i + half) % half) * nx) * rows, span) for i in range(2)
+            pl.multiple_of((which * slots + ((y_low - first - i + half + half // 2) % half) * nx) * rows, span) for i in range(2)
         ]
         left = jnp.concatenate([p_half[:, pl.ds(top, span)] for top in tops], axis=1)
 

time: 87.3 us -> 87.3 us (level)
  the two profiles are of different devices: /device:TPU:57 before, /device:TPU:3 now
where the time goes in v4:
time: 87.3 us; the launch traced here: 87 us
  Pallas kernels  84.7 us (97%)
  local copies, waits for them, and re-layouts  2.29 us (3%)
    pallas_call x1, Pallas kernels, local(): pl.pallas_call(functools.partial(kernel, nx, ny, nz, chunks), out_shape=j...  84.7 us
    unnamed x1, local copies, waits for them, and re-layouts  2.29 us

profile of v4, /device:TPU:3, one launch (start us, length us, event | category | flops | bytes accessed | tf_op | source)
XLA Modules:
  0.0 87.0 jit_solution(5651156871700971051)
XLA Ops:
  0.0 84.7 %precondition.1 = bf16[16,32,1024]{2,1,0:T(8,128)(2,1)} custom-call(s32[16]{0:T(128)} %slot_ref.1, bf16[16,32,1024]{2,1,0:T(8,128)(2,1)} %g_hbm.1, bf16[1,1024,1024]{2,1,0:T(8,128)(2,1)} %p_ref.1, bf16[1,64,1024]{2,1,0:T(8,128)(2,1)} %q_ref.1), custom_call_target="tpu_custom_call" | custom-call | flops 2147483648 | bytes 16777216 | tf_op jit(solution)/shard_map/precondition/pallas_call | solution.py:445
  84.7 2.3 %copy.6 = bf16[16,32,1024]{2,1,0:T(8,128)(2,1)} copy(bf16[16,32,1024]{2,1,0:T(8,128)(2,1)} %precondition.1) | data formatting | bytes 2097152
